TPU v7x, 512 devices: a whole 4x8x8 slice. The times are simulated.
512 devices in a mesh: section: 4 (over x), tensor: 16 (over z, y_lo), seq: 8 (over y_hi, core).
Axes of the slice: x: 4, y: 8 (y_hi: 4, y_lo: 2; y = y_hi * 2 + y_lo), z: 8, core: 2. Of those that a mesh axis runs over, the one named last changes fastest.
Arguments:
- stream: bfloat16 [4, 768, 6144], P('section', 'tensor', 'seq'), may hold values from -6 to 6
- norm_gain: float32 [4, 6144], P('section', 'seq'), may hold values from 0.5 to 1.5
- qkv_weight: bfloat16 [4, 6144, 3, 4096], P('section', 'seq', None, 'tensor'), may hold values from -0.078125 to 0.078125
- up_weight: bfloat16 [4, 6144, 12288], P('section', 'seq', 'tensor'), may hold values from -0.078125 to 0.078125
- out_weight: bfloat16 [4, 4096, 6144], P('section', 'tensor', 'seq'), may hold values from -0.375 to 0.375
- down_weight: bfloat16 [4, 12288, 6144], P('section', 'tensor', 'seq'), may hold values from -0.0546875 to 0.0546875
- slot_bias: float32 [4, 32, 27], P('section', 'tensor'), may hold values from -3 to 300
- neighbours: int32 [4, 24, 27], P('section', 'seq'), may hold values from 0 to 23, as said below
- present: int32 [4, 24, 27], P('section', 'seq'), may hold values from 0 to 1, as said below
- brick_slot: int32 [4, 24], P('section'), may hold values from 0 to 23, as said below
Outputs:
- stream_next: bfloat16 [4, 768, 6144], P('section', 'tensor', 'seq')
Inputs may be any that keep to these rules, and one draw needn't show every extreme that they name: `neighbours`: entry j of row r names the brick at offset j from the brick held in slot r (offsets -1, 0, 1 along each of three dimensions, the first slowest) when that place is occupied; otherwise its flag in present is 0 and it names the brick itself. Entry 13 is the brick itself. Flagged entries of a row are distinct. `present`: entry 13 of every row is 1. `brick_slot`: each section's row is a permutation of the 24 bricks.
All inputs are finite; a program needn't handle non-finite values.
Results may differ from a plain program's by a relative error of at most 0.025.
Values may be sent and summed in bfloat16 or wider, within the bound.
A program may use at most 64 MiB of HBM per device.

v0:
```python
import jax
import jax.numpy as jnp
from jax import lax
from jax.sharding import PartitionSpec as P

D = 6144
HEAD_DIM = 128
BRICK = 32


def passed_along(array, axis, by):
    peers = lax.axis_size(axis)
    return lax.ppermute(array, axis, [(i, (i + by) % peers) for i in range(peers)])


def attend_local(query_rows, keys_all, values_all, key_slots, flag_rows, head_bias):
    score_scale = HEAD_DIM ** (-0.5)
    heads_dev = head_bias.shape[0]
    bricks_dev = key_slots.shape[0]
    bricks_all = keys_all.shape[0] // BRICK
    query_bricks = query_rows.reshape(bricks_dev, BRICK, heads_dev, HEAD_DIM)
    key_bricks = keys_all.reshape(bricks_all, BRICK, heads_dev, HEAD_DIM)
    value_bricks = values_all.reshape(bricks_all, BRICK, heads_dev, HEAD_DIM)
    near_keys = key_bricks[key_slots]
    near_values = value_bricks[key_slots]
    scores = (
        jnp.einsum("rqhd,rjkhd->rhqjk", query_bricks, near_keys, preferred_element_type=jnp.float32)
        * score_scale
    )
    scores = scores + head_bias[None, :, None, :, None]
    usable = (flag_rows > 0)[:, None, None, :, None]
    largest = jnp.max(jnp.where(usable, scores, -1e30), axis=(3, 4), keepdims=True)
    exp_scores = jnp.where(usable, jnp.exp(scores - largest), 0.0)
    totals = jnp.sum(exp_scores, axis=(3, 4))
    weights = exp_scores.astype(jnp.bfloat16)
    mixed_sum = jnp.einsum(
        "rhqjk,rjkhd->rqhd", weights, near_values, preferred_element_type=jnp.float32
    )
    attended = mixed_sum / jnp.transpose(totals, (0, 2, 1))[:, :, :, None]
    return attended.astype(jnp.bfloat16).reshape(bricks_dev * BRICK, heads_dev * HEAD_DIM)


def per_device(
    stream,
    norm_gain,
    qkv_weight,
    up_weight,
    out_weight,
    down_weight,
    slot_bias,
    neighbours,
    present,
    brick_slot,
):
    stream_rows = stream[0]
    values = stream_rows.astype(jnp.float32)
    row_total, row_squares = lax.psum(
        (jnp.sum(values, axis=1), jnp.sum(values * values, axis=1)), "seq"
    )
    center = (row_total / D)[:, None]
    spread = (row_squares / D)[:, None] - center * center
    normed = ((values - center) * lax.rsqrt(spread + 1e-06) * norm_gain[0][None, :]).astype(
        jnp.bfloat16
    )
    gathered = lax.all_gather(normed, "tensor", axis=0, tiled=True)
    heads_dev = slot_bias.shape[1]
    width_dev = heads_dev * HEAD_DIM
    qkv_flat = qkv_weight[0].reshape(qkv_weight.shape[1], 3 * width_dev)
    up_block = up_weight[0]
    first_sums = lax.psum_scatter(
        jnp.concatenate(
            [
                jnp.dot(gathered, qkv_flat, preferred_element_type=jnp.float32),
                jnp.dot(gathered, up_block, preferred_element_type=jnp.float32),
            ],
            axis=1,
        ).astype(jnp.bfloat16),
        "seq",
        scatter_dimension=0,
        tiled=True,
    ).astype(jnp.float32)
    qkv_rows = first_sums[:, : 3 * width_dev].astype(jnp.bfloat16)
    hidden = jax.nn.gelu(first_sums[:, 3 * width_dev :], approximate=False).astype(jnp.bfloat16)
    keys_all, values_all = (
        lax.all_gather(qkv_rows[:, width_dev : 2 * width_dev], "seq", axis=0, tiled=True),
        lax.all_gather(qkv_rows[:, 2 * width_dev :], "seq", axis=0, tiled=True),
    )
    key_slots = brick_slot[0][neighbours[0]]
    attended = attend_local(
        qkv_rows[:, :width_dev], keys_all, values_all, key_slots, present[0], slot_bias[0]
    )
    joined_rows = jnp.concatenate([attended, hidden], axis=1)
    piece_rows = lax.all_gather(joined_rows, "seq", axis=0, tiled=True)
    partials = jnp.dot(
        piece_rows[:, :width_dev], out_weight[0], preferred_element_type=jnp.float32
    ) + jnp.dot(piece_rows[:, width_dev:], down_weight[0], preferred_element_type=jnp.float32)
    update = lax.psum_scatter(
        partials.astype(jnp.bfloat16), "tensor", scatter_dimension=0, tiled=True
    ).astype(jnp.float32)
    result = (values + update).astype(jnp.bfloat16)
    return passed_along(result[None], "section", 1)


def solution(mesh):
    return jax.shard_map(
        per_device,
        mesh=mesh,
        in_specs=(
            P("section", "tensor", "seq"),
            P("section", "seq"),
            P("section", "seq", None, "tensor"),
            P("section", "seq", "tensor"),
            P("section", "tensor", "seq"),
            P("section", "tensor", "seq"),
            P("section", "tensor", None),
            P("section", "seq", None),
            P("section", "seq", None),
            P("section", None),
        ),
        out_specs=P("section", "tensor", "seq"),
        check_vma=False,
    )
```

profile of v0, /device:TPU:16, one launch (start us, length us, event | category | flops | bytes accessed | tf_op | source)
XLA Modules:
  0.0 332.1 jit_solution(11792725883330970138)
XLA Ops:
  6.5 1.1 convert_reduce_fusion
  7.6 1.0 fusion.67
  8.6 15.6 %all-reduce = (f32[48]{0:T(128)S(1)}, f32[48]{0:T(128)S(1)}) all-reduce(f32[48]{0:T(128)S(1)} %fusion.67, f32[48]{0:T(128)S(1)} %convert_reduce_fusion), channel_id=1, replica_groups=mesh['section'=4,'tensor'=16,'seq'=8] {'seq'}, use_global_device_ids=true, to_apply=%region_3.0 | all-reduce | flops 96 | bytes 768 | tf_op jit(solution)/shard_map/psum | solution.py:57
  24.9 1.6 fusion.66
  26.6 1.6 copy.32
  28.2 75.2 %all-gather.3.cloned.1.call-done = bf16[768,768]{1,0:T(8,128)(2,1)} async-done(((bf16[48,768]{1,0:T(8,128)(2,1)}), bf16[768,768]{1,0:T(8,128)(2,1)}) %all-gather.3.cloned.1.call-update) | async-done | bytes 1179664 | tf_op jit(solution)/shard_map/all_gather | solution.py:65
  103.4 2.5 convolution_convert_fusion.1
  105.9 1.2 convolution_convert_fusion
  107.2 2.4 copy.50
  110.4 1.2 gather_fusion
  111.9 45.5 %reduce-scatter.7.cloned.1.call-done = bf16[96,1536]{1,0:T(8,128)(2,1)} async-done(((bf16[768,1536]{1,0:T(8,128)(2,1)}), bf16[96,1536]{1,0:T(8,128)(2,1)}) %reduce-scatter.7.cloned.1.call-update) | async-done | bytes 294928
  158.2 14.9 %all_gather.14 = bf16[768,256]{1,0:T(8,128)(2,1)S(1)} all-gather(bf16[96,256]{1,0:T(8,128)(2,1)S(1)} %get-tuple-element.8), channel_id=1, replica_groups=mesh['section'=4,'tensor'=16,'seq'=8] {'seq'}, dimensions={0}, use_global_device_ids=true | all-gather | bytes 442368 | tf_op jit(solution)/shard_map/all_gather | solution.py:85
  174.1 1.3 copy.42
  175.5 1.8 fusion.70
  178.8 14.8 %all_gather.13 = bf16[768,256]{1,0:T(8,128)(2,1)S(1)} all-gather(bf16[96,256]{1,0:T(8,128)(2,1)S(1)} %get-tuple-element.7), channel_id=1, replica_groups=mesh['section'=4,'tensor'=16,'seq'=8] {'seq'}, dimensions={0}, use_global_device_ids=true | all-gather | bytes 442368 | tf_op jit(solution)/shard_map/all_gather | solution.py:86
  194.6 2.7 fusion.23
  197.6 0.9 fusion.29
  199.5 34.4 %all-gather.5.cloned.1.call-done = bf16[768,1024]{1,0:T(8,128)(2,1)} async-done(((bf16[96,1024]{1,0:T(8,128)(2,1)}), bf16[768,1024]{1,0:T(8,128)(2,1)}) %all-gather.5.cloned.1.call-update) | async-done | bytes 1572880 | tf_op jit(solution)/shard_map/all_gather | solution.py:93
  233.9 2.7 fusion.9
  236.6 2.5 add_convert_fusion
  239.2 77.4 %reduce-scatter.5.cloned.1.call-done = bf16[48,768]{1,0:T(8,128)(2,1)} async-done(((bf16[768,768]{1,0:T(8,128)(2,1)}), bf16[48,768]{1,0:T(8,128)(2,1)}) %reduce-scatter.5.cloned.1.call-update) | async-done | bytes 73744 | tf_op jit(solution)/shard_map/reduce_scatter | solution.py:97
  316.6 0.9 fusion.69
  317.5 3.3 collective-permute-start
  320.8 4.2 %collective-permute-done = bf16[1,48,768]{2,1,0:T(8,128)(2,1)S(1)} collective-permute-done((bf16[1,48,768]{2,1,0:T(8,128)(2,1)S(1)}, bf16[1,48,768]{2,1,0:T(8,128)(2,1)S(1)}, u32[]{:S(2)}, u32[]{:S(2)}) %collective-permute-start) | collective-permute-done | bytes 73760 | tf_op jit(solution)/shard_map/ppermute | solution.py:13
  (57 shorter events, 8.2 us)
Async XLA Ops:
  6.5 99.3 %copy-start = (bf16[1,768,768]{2,1,0:T(8,128)(2,1)S(1)}, bf16[1,768,768]{2,1,0:T(8,128)(2,1)}, u32[]{:S(2)}) copy-start(bf16[1,768,768]{2,1,0:T(8,128)(2,1)} %param.13) | copy-start | bytes 3538948
  6.5 96.8 %all-gather.3.cloned.1.call-start = ((), (), s32[]{:S(2)}) async-start(), calls=%async_computation.2 | async-start | bytes 1253376 | tf_op jit(solution)/shard_map/all_gather | solution.py:65
  26.6 130.8 %reduce-scatter.7.cloned.1.call-start = ((), (), s32[]{:S(2)}) async-start(), calls=%async_computation.5 | async-start | bytes 2654208
  103.3 2.5 copy-start.8
  109.6 0.7 copy-start.6
  109.6 0.8 copy-start.1
  109.6 2.2 copy-start.7
  109.7 124.2 %all-gather.5.cloned.1.call-start = ((), (), s32[]{:S(2)}) async-start(), calls=%async_computation.3 | async-start | bytes 1769472 | tf_op jit(solution)/shard_map/all_gather | solution.py:93
  175.4 1.8 copy-start.5
  177.3 1.5 copy-start.2
  194.5 2.9 slice-start
  199.4 37.2 %copy-start.4 = (bf16[1,256,768]{2,1,0:T(8,128)(2,1)S(1)}, bf16[1,256,768]{2,1,0:T(8,128)(2,1)}, u32[]{:S(2)}) copy-start(bf16[1,256,768]{2,1,0:T(8,128)(2,1)} %param.14) | copy-start | bytes 1179652
  199.4 117.1 %reduce-scatter.5.cloned.1.call-start = ((), (), s32[]{:S(2)}) async-start(), calls=%async_computation.4 | async-start | bytes 1253376 | tf_op jit(solution)/shard_map/reduce_scatter | solution.py:97
  236.6 80.0 %copy-start.3 = (bf16[1,48,768]{2,1,0:T(8,128)(2,1)S(1)}, bf16[1,48,768]{2,1,0:T(8,128)(2,1)}, u32[]{:S(2)}) copy-start(bf16[1,48,768]{2,1,0:T(8,128)(2,1)} %param.10) | copy-start | bytes 221188
  317.5 7.5 %collective-permute-start = (bf16[1,48,768]{2,1,0:T(8,128)(2,1)S(1)}, bf16[1,48,768]{2,1,0:T(8,128)(2,1)S(1)}, u32[]{:S(2)}, u32[]{:S(2)}) collective-permute-start(bf16[1,48,768]{2,1,0:T(8,128)(2,1)S(1)} %fusion.69), channel_id=1, source_target_pairs={{0,128},{128,256},{256,384},{384,0},{1,129},{129,257},{257,385},{3... | collective-permute-start | bytes 221192 | tf_op jit(solution)/shard_map/ppermute | solution.py:13
Sparse Core Ops, SparseCore 0:
  26.7 76.6 all-gather.2
  109.8 47.5 reduce-scatter.6
  199.5 34.3 all-gather.4
  239.3 77.2 reduce-scatter.4
where the time goes:
time: 333 us; the launch traced here: 332 us
  waiting for transfers between devices  237 us (71%)
  blocking collectives  45.2 us (14%)
  matrix products  13.4 us (4%)
  between operations  13.4 us (4%)
  local copies, waits for them, and re-layouts  12.1 us (4%)
  other arithmetic  7.84 us (2%)
  starting transfers between devices  3.42 us (1%)
    reduce_scatter x1, waiting for transfers between devices, per_device(): lax.psum_scatter(partials.astype(jnp.bfloat16), 'tensor', scatter_dimensi...  77.4 us
    all_gather x1, waiting for transfers between devices, per_device(): gathered = lax.all_gather(normed, 'tensor', axis=0, tiled=True)  75.2 us
    unnamed x5, waiting for transfers between devices  45.5 us
    all_gather x1, waiting for transfers between devices, per_device(): piece_rows = lax.all_gather(joined_rows, 'seq', axis=0, tiled=True)  34.4 us
    psum x1, blocking collectives, per_device(): lax.psum((jnp.sum(values, axis=1), jnp.sum(values * values, axis=1)), 'seq')  15.6 us
    all_gather x1, blocking collectives, per_device(): lax.all_gather(qkv_rows[:, width_dev:2 * width_dev], 'seq', axis=0, tiled...  14.9 us
    all_gather x1, blocking collectives, per_device(): lax.all_gather(qkv_rows[:, 2 * width_dev:], 'seq', axis=0, tiled=True)  14.8 us
  transfers between devices with their start and end apart: 5, of which 5 were waited for; matrix products, arithmetic and copies ran while one was open for 1% of the time, Pallas kernels for 0%

commit v1 on v0

v1 whole, which is shorter than its diff:
```python
import functools
import math

import jax
import jax.numpy as jnp
from jax import lax
from jax.experimental import pallas as pl
from jax.experimental.pallas import tpu as pltpu
from jax.sharding import PartitionSpec as P

HD = 128
BRICK = 32
NBR = 27
RINGZ = 8
CHIPS = 4
MESH = pl.DeviceIdType.MESH
F32 = jnp.float32
BF16 = jnp.bfloat16


def _dot(a, b):
    return jnp.dot(a, b, preferred_element_type=F32)


def kernel(
    dims,
    x_in, gain_in, qkv_in, up_in, out_in, down_in, nb_in, pr_in, bs_in, sb_ref,
    o_ref,
    xv, gain, w1q, w1u, w2, nbv, prv, bsv,
    st_t, st_snd, st_rcv, tab, bias,
    xg,
    psq, psu, rsq, rsu, poq, pou, soq, sou, roq, rou, nsq, nsu, rnq, rnu,
    qb, kvb, jb,
    fown, es3, es, er, lsnd, lrcv, res,
    sem_loc, sem_st, sem_tab, sem_a, sem_sib, sem_o, sem_n, sem_kv, sem_d, sem_df, sem_e, sem_l, sem_sec,
):
    RB, FD, UC, CO, BPD, DW, SECT = dims
    AH = HD + UC
    PB = CHIPS * RB
    sect = lax.axis_index("section")
    tens = lax.axis_index("tensor")
    seq = lax.axis_index("seq")
    z, l = lax.div(tens, 2), lax.rem(tens, 2)
    i, c = lax.div(seq, 2), lax.rem(seq, 2)
    zp = {"tensor": lax.rem(z + 1, RINGZ) * 2 + l}
    zm = {"tensor": lax.rem(z + RINGZ - 1, RINGZ) * 2 + l}
    lp = {"tensor": z * 2 + 1 - l}
    ip = lax.rem(i + 1, CHIPS)
    im = lax.rem(i + 3, CHIPS)
    io = lax.rem(i + 2, CHIPS)
    dp = {"seq": ip * 2 + c}
    dm = {"seq": im * 2 + c}
    sib = {"seq": i * 2 + 1 - c}
    sec_next = {"section": lax.rem(sect + 1, SECT)}
    sec_prev = {"section": lax.rem(sect + SECT - 1, SECT)}

    sends = []

    def rcopy(src, dst, sem, dev):
        return pltpu.make_async_remote_copy(
            src_ref=src, dst_ref=dst, send_sem=sem.at[0], recv_sem=sem.at[1],
            device_id=dev, device_id_type=MESH,
        )

    def send(src, dst, sem, dev):
        d = rcopy(src, dst, sem, dev)
        d.start()
        sends.append(d)

    def recv(dst, sem, dev):
        rcopy(dst, dst, sem, dev).wait_recv()

    loads = []

    def load(src, dst):
        d = pltpu.make_async_copy(src, dst, sem_loc.at[len(loads)])
        d.start()
        loads.append(d)
        return d

    ld_x = load(x_in, xv)
    ld_g = load(gain_in, gain)
    ld_t = [load(nb_in, nbv), load(pr_in, prv), load(bs_in, bsv)]
    ld_w = []
    for hf in range(2):
        cc = c if hf == 0 else 1 - c
        hcol = pl.ds(pl.multiple_of(cc * HD, HD), HD)
        ucol = pl.ds(pl.multiple_of(cc * UC, HD), UC)
        for g in range(3):
            ld_w.append(load(qkv_in.at[g, :, hcol], w1q.at[hf, :, g * HD : (g + 1) * HD]))
        ld_w.append(load(up_in.at[:, ucol], w1u.at[hf]))
    ld_w2 = []
    for hf in range(2):
        cc = c if hf == 0 else 1 - c
        ld_w2.append(load(out_in.at[pl.ds(pl.multiple_of(cc * HD, HD), HD), :], w2.at[hf, 0:HD]))
        ld_w2.append(load(down_in.at[pl.ds(pl.multiple_of(cc * UC, HD), UC), :], w2.at[hf, HD:AH]))

    barrier = pltpu.get_barrier_semaphore()
    peers = []
    for k in range(1, 8):
        peers.append({"seq": lax.rem(seq + k, 8)})
    greet = peers + [zp, zm, lp] + ([sec_prev] if SECT > 1 else [])
    for dev in greet:
        pl.semaphore_signal(barrier, inc=1, device_id=dev, device_id_type=MESH)

    ld_x.wait()
    xf = xv[...].astype(F32)
    s1 = jnp.sum(xf, axis=1, keepdims=True)
    s2 = jnp.sum(xf * xf, axis=1, keepdims=True)
    lane = lax.broadcasted_iota(jnp.int32, (RB, 128), 1)
    st_t[...] = jnp.zeros((128, 128), F32)
    st_t[0:RB, :] = jnp.where(lane == 0, s1, jnp.where(lane == 1, s2, 0.0))
    st_snd[...] = st_t[...].T[0:8, :]
    for d in ld_t:
        d.wait()
    tab[0] = jnp.full((8, 128), -1, jnp.int32)
    for q in range(BPD):
        tab[0, q : q + 1, 0:NBR] = jnp.where(prv[q] > 0, nbv[q], -1)
    pl.semaphore_wait(barrier, len(greet))
    for k in range(1, 8):
        send(st_snd, st_rcv.at[k - 1], sem_st.at[k - 1], peers[k - 1])
    for k in range(1, 8):
        send(tab.at[0], tab.at[k], sem_tab.at[k - 1], peers[k - 1])
    tot = st_snd[...]
    for k in range(1, 8):
        recv(st_rcv.at[k - 1], sem_st.at[k - 1], peers[k - 1])
        tot = tot + st_rcv[k - 1]
    st_t[0:8, :] = tot * (1.0 / DW)
    cols = st_t[...].T
    mean = cols[0:RB, 0:1]
    sq = cols[0:RB, 1:2]
    ld_g.wait()
    normed = (xf - mean) * lax.rsqrt(sq - mean * mean + 1e-06) * gain[...]
    xg[0, 0:RB] = normed.astype(BF16)

    def slot(m, sgn, lr):
        lo = RB * (2 * sgn + lr)
        return xg.at[m, lo : lo + RB]

    def a_sem(m, sgn, lr):
        return sem_a.at[m * 4 + sgn * 2 + lr]

    def a_send(src, dst, dev):
        send(slot(*src), slot(*dst), a_sem(*dst), dev)

    def a_recv(*dst):
        recv(slot(*dst), a_sem(*dst), zp)

    a_send((0, 0, 0), (0, 0, 1), lp)
    a_send((0, 0, 0), (1, 1, 0), zp)
    a_send((0, 0, 0), (1, 0, 0), zm)
    a_recv(0, 0, 1)
    a_send((0, 0, 1), (1, 1, 1), zp)
    a_send((0, 0, 1), (1, 0, 1), zm)

    def token_of(m, j, row):
        sgn, lr = lax.shift_right_logical(j, 1), lax.bitwise_and(j, 1)
        zo = jnp.where(m == 0, 4 * sgn, jnp.where(sgn == 0, m, RINGZ - m))
        zz = lax.bitwise_and(zo + z, RINGZ - 1)
        ll = lax.bitwise_and(lr + l, 1)
        return (2 * zz + ll) * RB + row

    def blocks(k):
        b = lax.shift_right_logical(k * (65536 // RB + 1), 16)
        return b, k - b * RB

    KEYS = 4 * PB
    QROWS = 4 * RB
    for k in range(1, 8):
        recv(tab.at[k], sem_tab.at[k - 1], peers[k - 1])
    enc = tab[...].reshape(64, 128)
    brick_id = lax.broadcasted_iota(jnp.int32, (64, 128), 1)
    near = jnp.full((64, 128), -1e30, F32)
    for j in range(NBR):
        near = jnp.where(enc[:, j : j + 1] == brick_id, sb_ref[c, j], near)
    key_i = lax.broadcasted_iota(jnp.int32, (1, KEYS), 1)
    kb, krow = blocks(key_i)
    kslot = lax.shift_right_logical(
        token_of(lax.shift_right_logical(kb, 2), lax.bitwise_and(kb, 3), krow), 5
    )
    eye = lax.broadcasted_iota(jnp.int32, (128, 128), 0) == lax.broadcasted_iota(
        jnp.int32, (128, 128), 1
    )
    bs_row = jnp.pad(bsv[...], ((0, 0), (0, 128 - 8 * BPD)), constant_values=-1).astype(F32)
    bs_col = jnp.sum(jnp.where(eye, bs_row, 0.0), axis=1, keepdims=True).astype(jnp.int32)
    of_key = jnp.where(bs_col == kslot, 1.0, 0.0)
    near_keys = jnp.dot(near, of_key, precision=lax.Precision.HIGHEST, preferred_element_type=F32)
    q_i = lax.broadcasted_iota(jnp.int32, (QROWS, 1), 0)
    qm, qrow = blocks(q_i)
    qslot = lax.shift_right_logical(token_of(qm, i + jnp.zeros_like(qm), qrow), 5)
    qdev = lax.shift_right_logical(qslot * (512 // BPD + 1), 9)
    qpos = 8 * lax.bitwise_and(seq + 8 - qdev, 7) + (qslot - BPD * qdev)
    of_query = jnp.where(qpos == lax.broadcasted_iota(jnp.int32, (1, 64), 1), 1.0, 0.0)
    bias[...] = jnp.dot(
        of_query, near_keys, precision=lax.Precision.HIGHEST, preferred_element_type=F32
    )

    ps, rs, po = (psq, psu), (rsq, rsu), (poq, pou)
    so, ro, ns, rn = (soq, sou), (roq, rou), (nsq, nsu), (rnq, rnu)
    w1 = (w1q, w1u)

    def rows(j):
        return pl.ds(pl.multiple_of(j * RB, 16), RB)

    def gather_stage(m):
        if m == 0:
            a_recv(0, 1, 0)
            a_recv(0, 1, 1)
            return
        for lr in range(2):
            for sgn in range(2):
                a_recv(m, sgn, lr)
                dev = zp if sgn == 1 else zm
                if m < 3:
                    a_send((m, sgn, lr), (m + 1, sgn, lr), dev)
                elif lr == sgn:
                    a_send((3, sgn, lr), (0, 1, lr), dev)

    def project(p, m):
        ps[p][m] = _dot(xg[m], w1[p][1]).astype(BF16)
        send(ps[p].at[m], rs[p].at[m], sem_sib.at[p, m], sib)
        po[p][m] = _dot(xg[m], w1[p][0])
        recv(rs[p].at[m], sem_sib.at[p, m], sib)
        so[p][m] = (po[p][m, rows(io), :] + rs[p][m, rows(io), :].astype(F32)).astype(BF16)
        send(so[p].at[m], ro[p].at[m], sem_o.at[p, m], dp if m % 2 == 0 else dm)

    def relay(p, m):
        recv(ro[p].at[m], sem_o.at[p, m], dp)
        for d, (j, dev) in enumerate(((ip, dp), (im, dm))):
            v = po[p][m, rows(j), :] + rs[p][m, rows(j), :].astype(F32)
            if d == m % 2:
                v = v + ro[p][m].astype(F32)
            ns[p][d, m] = v.astype(BF16)
            send(ns[p].at[d, m], rn[p].at[d, m], sem_n.at[p, d, m], dev)

    def reduced(p, m):
        v = po[p][m, rows(i), :] + rs[p][m, rows(i), :].astype(F32)
        for d in range(2):
            recv(rn[p].at[d, m], sem_n.at[p, d, m], dp)
            v = v + rn[p][d, m].astype(F32)
        return v

    def kv_rows(m, j):
        return kvb.at[pl.ds(pl.multiple_of(m * PB + j * RB, 16), RB)]

    def finish_qkv(m):
        v = reduced(0, m).astype(BF16)
        qb[m] = v[:, 0:HD]
        own = kv_rows(m, i)
        own[...] = v[:, HD:]
        send(own, own, sem_kv.at[m, 0], dp)
        send(own, own, sem_kv.at[m, 1], dm)

    def kv_relay(m):
        recv(kv_rows(m, im), sem_kv.at[m, 0], dp)
        recv(kv_rows(m, ip), sem_kv.at[m, 1], dp)
        j, dev = (im, dp) if m % 2 == 0 else (ip, dm)
        send(kv_rows(m, j), kv_rows(m, j), sem_kv.at[m, 2], dev)

    span = ((0, HD), (HD, AH))

    def j_part(hf, part, m, j):
        return jb.at[hf, m, rows(j), span[part][0] : span[part][1]]

    def spread(part, m):
        own = j_part(0, part, m, i)
        send(own, own, sem_d.at[part, m, 0], dp)
        send(own, own, sem_d.at[part, m, 1], dm)
        send(own, j_part(1, part, m, i), sem_df.at[part, m, 0], sib)

    def spread_relay(part, m):
        for d, j in enumerate((im, ip)):
            got = j_part(0, part, m, j)
            recv(got, sem_d.at[part, m, d], dp)
            if d == m % 2:
                send(got, got, sem_d.at[part, m, 2], dp if d == 0 else dm)
            send(got, j_part(1, part, m, j), sem_df.at[part, m, 1 + d], sib)

    def spread_last(part, m):
        got = j_part(0, part, m, io)
        recv(got, sem_d.at[part, m, 2], dp)
        send(got, j_part(1, part, m, io), sem_df.at[part, m, 3], sib)

    def spread_sib(part, m):
        for k, j in enumerate((i, im, ip, io)):
            recv(j_part(1, part, m, j), sem_df.at[part, m, k], sib)

    def finish_up(m):
        u = reduced(1, m)
        h = u * (1.0 + lax.erf(u * (1.0 / math.sqrt(2.0)))) * 0.5
        jb[0, m, rows(i), HD:AH] = h.astype(BF16)
        spread(1, m)

    def attend():
        for m in range(4):
            recv(kv_rows(m, io), sem_kv.at[m, 2], dp)
        for m in range(4):
            s = lax.dot_general(
                qb[m], kvb[:, 0:HD], (((1,), (1,)), ((), ())), preferred_element_type=F32
            )
            s = s * (HD**-0.5) + bias[m * RB : (m + 1) * RB, :]
            e = jnp.exp(s - jnp.max(s, axis=1, keepdims=True))
            total = jnp.sum(e, axis=1, keepdims=True)
            a = _dot(e.astype(BF16), kvb[:, HD:]) / total
            jb[0, m, rows(i), 0:HD] = a.astype(BF16)
            spread(0, m)

    def contribute(m):
        for part in range(2):
            spread_last(part, m)
        f = _dot(jb[0, m], w2[0])
        for part in range(2):
            spread_sib(part, m)
        f = f + _dot(jb[1, m], w2[1])
        if m == 0:
            fown[...] = f[0 : 2 * RB]
            es3[...] = f[2 * RB :].astype(BF16)
            for lr, dev in ((0, zp), (1, zm)):
                blk = es3.at[lr * RB : (lr + 1) * RB]
                send(blk, er.at[3, lr, lr * RB : (lr + 1) * RB], sem_e.at[3, lr], dev)
            return
        for sgn, dev in ((0, zp), (1, zm)):
            v = f[2 * RB * sgn : 2 * RB * (sgn + 1)]
            if m == 3:
                lo = sgn * RB
                recv(er.at[3, sgn, lo : lo + RB], sem_e.at[3, sgn], dev)
                es[m - 1, sgn, lo : lo + RB] = (
                    v[lo : lo + RB] + er[3, sgn, lo : lo + RB].astype(F32)
                ).astype(BF16)
                no = RB - lo
                es[m - 1, sgn, no : no + RB] = v[no : no + RB].astype(BF16)
            else:
                recv(er.at[m, sgn], sem_e.at[m, sgn], dev)
                es[m - 1, sgn] = (v + er[m, sgn].astype(F32)).astype(BF16)
            send(es.at[m - 1, sgn], er.at[m - 1, sgn], sem_e.at[m - 1, sgn], dev)

    def last():
        for sgn in range(2):
            recv(er.at[0, sgn], sem_e.at[0, sgn], zp)
        v = fown[...] + er[0, 0].astype(F32) + er[0, 1].astype(F32)
        lsnd[...] = v[RB:].astype(BF16)
        send(lsnd, lrcv, sem_l, lp)
        base = xv[...].astype(F32) + v[0:RB]
        recv(lrcv, sem_l, lp)
        res[...] = (base + lrcv[...].astype(F32)).astype(BF16)
        if SECT > 1:
            send(res, o_ref, sem_sec, sec_next)
        else:
            d = pltpu.make_async_copy(res, o_ref, sem_loc.at[0])
            d.start()
            d.wait()

    gather_stage(1)
    for d in ld_w:
        d.wait()
    project(0, 1)
    gather_stage(2)
    project(0, 2)
    relay(0, 1)
    gather_stage(3)
    project(0, 3)
    relay(0, 2)
    finish_qkv(1)
    gather_stage(0)
    project(0, 0)
    relay(0, 3)
    finish_qkv(2)
    project(1, 0)
    relay(0, 0)
    finish_qkv(3)
    kv_relay(1)
    project(1, 3)
    relay(1, 0)
    finish_qkv(0)
    kv_relay(2)
    project(1, 2)
    relay(1, 3)
    kv_relay(3)
    finish_up(0)
    project(1, 1)
    kv_relay(0)
    relay(1, 2)
    finish_up(3)
    attend()
    relay(1, 1)
    spread_relay(1, 0)
    finish_up(2)
    for m in (0, 3, 2, 1):
        spread_relay(0, m)
    spread_relay(1, 3)
    finish_up(1)
    for d in ld_w2:
        d.wait()
    contribute(0)
    spread_relay(1, 2)
    contribute(3)
    spread_relay(1, 1)
    contribute(2)
    contribute(1)
    last()
    for d in sends:
        d.wait_send()
    if SECT > 1:
        recv(o_ref, sem_sec, sec_next)


def per_device(sect, x, gain, qkv, up, out, down, sb, nb, pr, bs):
    RB, FD = x.shape[1:]
    UC = up.shape[2] // 2
    CO = out.shape[2]
    BPD = nb.shape[1]
    AH = HD + UC
    PB = CHIPS * RB
    QC = 3 * HD
    dims = (RB, FD, UC, CO, BPD, FD * 8, sect)
    vm, sm = pltpu.VMEM, pltpu.SemaphoreType.DMA
    scratch = [
        vm((RB, FD), BF16), vm((1, FD), F32), vm((2, FD, QC), BF16), vm((2, FD, UC), BF16),
        vm((2, AH, CO), BF16),
        vm((BPD, 1, NBR), jnp.int32), vm((BPD, 1, NBR), jnp.int32), vm((1, 8 * BPD), jnp.int32),
        vm((128, 128), F32), vm((8, 128), F32), vm((7, 8, 128), F32), vm((8, 8, 128), jnp.int32),
        vm((4 * RB, 4 * PB), F32),
        vm((4, PB, FD), BF16),
    ]
    two = (QC, UC)
    scratch += [vm((4, PB, w), BF16) for w in two]
    scratch += [vm((4, PB, w), BF16) for w in two]
    scratch += [vm((4, PB, w), F32) for w in two]
    scratch += [vm((4, RB, w), BF16) for w in two]
    scratch += [vm((4, RB, w), BF16) for w in two]
    scratch += [vm((2, 4, RB, w), BF16) for w in two]
    scratch += [vm((2, 4, RB, w), BF16) for w in two]
    scratch += [
        vm((4, RB, HD), BF16), vm((4 * PB, 2 * HD), BF16), vm((2, 4, PB, AH), BF16),
        vm((2 * RB, CO), F32), vm((2 * RB, CO), BF16), vm((3, 2, 2 * RB, CO), BF16),
        vm((4, 2, 2 * RB, CO), BF16), vm((RB, CO), BF16), vm((RB, CO), BF16), vm((RB, CO), BF16),
        sm((20,)), sm((7, 2)), sm((7, 2)), sm((16, 2)), sm((2, 4, 2)), sm((2, 4, 2)),
        sm((2, 2, 4, 2)), sm((4, 3, 2)), sm((2, 4, 3, 2)), sm((2, 4, 4, 2)), sm((4, 2, 2)),
        sm((2,)), sm((2,)),
    ]
    hbm = pl.BlockSpec(memory_space=pl.ANY)
    y = pl.pallas_call(
        functools.partial(kernel, dims),
        out_shape=jax.ShapeDtypeStruct((RB, CO), BF16),
        in_specs=[hbm] * 9 + [pl.BlockSpec(memory_space=pltpu.SMEM)],
        out_specs=hbm,
        scratch_shapes=scratch,
        compiler_params=pltpu.CompilerParams(
            collective_id=0, has_side_effects=True, vmem_limit_bytes=56 * 2**20
        ),
    )(
        x[0], gain, jnp.transpose(qkv[0], (1, 0, 2)), up[0], out[0], down[0],
        jnp.transpose(nb, (1, 0, 2)), jnp.transpose(pr, (1, 0, 2)), bs, sb[0],
    )
    return y[None]


def solution(mesh):
    return jax.shard_map(
        functools.partial(per_device, mesh.shape["section"]),
        mesh=mesh,
        in_specs=(
            P("section", "tensor", "seq"),
            P("section", "seq"),
            P("section", "seq", None, "tensor"),
            P("section", "seq", "tensor"),
            P("section", "tensor", "seq"),
            P("section", "tensor", "seq"),
            P("section", "tensor", None),
            P("section", "seq", None),
            P("section", "seq", None),
            P("section", None),
        ),
        out_specs=P("section", "tensor", "seq"),
        check_vma=False,
    )
```

time: 333 us -> 105 us (0.32)
  waiting for transfers between devices: 237 us -> 0 us
  Pallas kernels: 0 us -> 104 us
  blocking collectives: 45.2 us -> 0 us
  matrix products: 13.4 us -> 0 us
  between operations: 13.4 us -> 0.01 us
  local copies, waits for them, and re-layouts: 12.1 us -> 1.52 us
  other arithmetic: 7.84 us -> 0 us
  starting transfers between devices: 3.42 us -> 0 us
    all_gather x2 -> x0, waiting for transfers between devices: 110 us -> none  [the longest x1 75.2 us: per_device(): gathered = lax.all_gather(normed, 'tensor', axis=0, tiled=True)]
    pallas_call x0 -> x1, Pallas kernels: none -> 104 us  [per_device(): pl.pallas_call(functools.partial(kernel, dims), out_shape=jax.ShapeDtypeS...]
    reduce_scatter x1 -> x0, waiting for transfers between devices: 77.4 us -> none  [per_device(): lax.psum_scatter(partials.astype(jnp.bfloat16), 'tensor', scatter_dimensi...]
    unnamed x5 -> x0, waiting for transfers between devices: 45.5 us -> none
    all_gather x2 -> x0, blocking collectives: 29.7 us -> none  [the longest x1 14.9 us: per_device(): lax.all_gather(qkv_rows[:, width_dev:2 * width_dev], 'seq', axis=0, tiled...]
    psum x1 -> x0, blocking collectives: 15.6 us -> none  [per_device(): lax.psum((jnp.sum(values, axis=1), jnp.sum(values * values, axis=1)), 'seq')]
    dot_general x5 -> x0, matrix products: 11.6 us -> none  [the longest x1 2.72 us: attend_local(): jnp.einsum('rhqjk,rjkhd->rqhd', weights, near_values, preferred_element_t...]
    gather x5 -> x0, local copies, waits for them, and re-layouts: 4.22 us -> none  [the longest x2 2.11 us: attend_local(): near_keys = key_bricks[key_slots]]
  transfers between devices with their start and end apart: 5 -> 0, of which waited for: 5 -> 0; matrix products, arithmetic and copies ran while one was open for 1% -> 0% of each run, Pallas kernels for 0% -> 0%
where the time goes in v1:
time: 105 us
  Pallas kernels  104 us (99%)
  local copies, waits for them, and re-layouts  1.52 us (1%)
    pallas_call x1, Pallas kernels, per_device(): pl.pallas_call(functools.partial(kernel, dims), out_shape=jax.ShapeDtypeS...  104 us

profile of v1, /device:TPU:16, one launch (start us, length us, event | category | flops | bytes accessed | tf_op | source)
XLA Modules:
  0.0 105.1 jit_solution(3315922047482671165)
XLA Ops:
  0.0 103.6 %shard_map.100 = bf16[48,768]{1,0:T(8,128)(2,1)} custom-call(bf16[48,768]{1,0:T(8,128)(2,1)} %bitcast.16, f32[1,768]{1,0:T(1,128)} %gain_in.1, bf16[3,768,256]{2,1,0:T(8,128)(2,1)} %bitcast.11, bf16[768,768]{1,0:T(8,128)(2,1)} %bitcast.12, bf16[256,768]{1,0:T(8,128)(2,1)} %bitcast.14, bf16[768,768]{1,0:T(8,128)(2,1)} %bitcast.13, s32[3,1,27]{2,1,0:T(1,128)} %bitcast.17, ...), custom_call_target="tpu_custom_call" | custom-call | tf_op jit(solution)/shard_map/pallas_call | solution.py:442
  103.6 1.5 %copy.12 = bf16[1,48,768]{2,1,0:T(8,128)(2,1)} copy(bf16[1,48,768]{2,1,0:T(8,128)(2,1)} %bitcast.15) | data formatting | bytes 147456

commit v2 on v1

v2 whole, which is shorter than its diff:
```python
import functools
import math

import jax
import jax.numpy as jnp
from jax import lax
from jax.experimental import pallas as pl
from jax.experimental.pallas import tpu as pltpu
from jax.sharding import PartitionSpec as P

HD = 128
BRICK = 32
NBR = 27
RINGZ = 8
CHIPS = 4
MESH = pl.DeviceIdType.MESH
F32 = jnp.float32
BF16 = jnp.bfloat16


def _dot(a, b):
    return jnp.dot(a, b, preferred_element_type=F32)


def kernel(
    dims,
    x_in, gain_in, qkv_in, up_in, out_in, down_in, nb_in, pr_in, bs_in, sb_ref,
    o_ref,
    xv, gain, w1q, w1u, w2, nbv, prv, bsv,
    st_t, st_grp, st_own, st_all, bias,
    xg, gvs, gvg, gm, xc,
    psq, psu, rsq, rsu, poq, pou, sou, rou, nsq, nsu, rnq, rnu,
    qb, kvb, jb,
    fown, fbuf, es3, es, er, fin, lsnd, lrcv, res,
    sem_loc, sem_st, sem_g, sem_all, sem_a, sem_sib, sem_o, sem_n, sem_kv, sem_d, sem_df, sem_e, sem_f, sem_l, sem_sec,
):
    RB, FD, UC, CO, BPD, DW, SECT = dims
    AH = HD + UC
    PB = CHIPS * RB
    sect = lax.axis_index("section")
    tens = lax.axis_index("tensor")
    seq = lax.axis_index("seq")
    z, l = lax.div(tens, 2), lax.rem(tens, 2)
    i, c = lax.div(seq, 2), lax.rem(seq, 2)
    zp = {"tensor": lax.rem(z + 1, RINGZ) * 2 + l}
    zm = {"tensor": lax.rem(z + RINGZ - 1, RINGZ) * 2 + l}
    zpo = {"tensor": lax.rem(z + 1, RINGZ) * 2 + 1 - l}
    zmo = {"tensor": lax.rem(z + RINGZ - 1, RINGZ) * 2 + 1 - l}
    lp = {"tensor": z * 2 + 1 - l}
    ip = lax.rem(i + 1, CHIPS)
    im = lax.rem(i + 3, CHIPS)
    io = lax.rem(i + 2, CHIPS)
    dp = {"seq": ip * 2 + c}
    dm = {"seq": im * 2 + c}
    do = {"seq": io * 2 + c}
    sib = {"seq": i * 2 + 1 - c}
    sec_next = {"section": lax.rem(sect + 1, SECT)}
    sec_prev = {"section": lax.rem(sect + SECT - 1, SECT)}

    sends = []

    def rcopy(src, dst, sem, dev):
        return pltpu.make_async_remote_copy(
            src_ref=src, dst_ref=dst, send_sem=sem.at[0], recv_sem=sem.at[1],
            device_id=dev, device_id_type=MESH,
        )

    def send(src, dst, sem, dev):
        d = rcopy(src, dst, sem, dev)
        d.start()
        sends.append(d)

    def recv(dst, sem, dev):
        rcopy(dst, dst, sem, dev).wait_recv()

    loads = []

    def load(src, dst):
        d = pltpu.make_async_copy(src, dst, sem_loc.at[len(loads)])
        d.start()
        loads.append(d)
        return d

    ld_x = load(x_in, xv)
    ld_g = load(gain_in, gain)
    ld_t = [load(nb_in, nbv), load(pr_in, prv), load(bs_in, bsv)]
    ld_w = []
    for hf in range(2):
        cc = c if hf == 0 else 1 - c
        hcol = pl.ds(pl.multiple_of(cc * HD, HD), HD)
        ucol = pl.ds(pl.multiple_of(cc * UC, HD), UC)
        for g in range(3):
            ld_w.append(load(qkv_in.at[g, :, hcol], w1q.at[hf, :, g * HD : (g + 1) * HD]))
        ld_w.append(load(up_in.at[:, ucol], w1u.at[hf]))
    ld_w2 = []
    for hf in range(2):
        cc = c if hf == 0 else 1 - c
        ld_w2.append(load(out_in.at[pl.ds(pl.multiple_of(cc * HD, HD), HD), :], w2.at[hf, 0:HD]))
        ld_w2.append(load(down_in.at[pl.ds(pl.multiple_of(cc * UC, HD), UC), :], w2.at[hf, HD:AH]))

    barrier = pltpu.get_barrier_semaphore()
    peers = [{"seq": lax.rem(seq + k, 8)} for k in range(1, 8)]
    kin = []
    for dz in range(RINGZ):
        for lr in range(2):
            if dz + lr:
                zz = lax.rem(z + dz, RINGZ)
                dev = {"tensor": zz * 2 + (l if lr == 0 else 1 - l)}
                place = (0, 1) if dz == 4 else (dz, 1) if dz < 4 else (RINGZ - dz, 0)
                kin.append((dev, place + (lr,) if dz else (0, 0, lr)))
    greet = peers + [dev for dev, _ in kin] + ([sec_prev] if SECT > 1 else [])
    for dev in greet:
        pl.semaphore_signal(barrier, inc=1, device_id=dev, device_id_type=MESH)

    ld_x.wait()
    ld_g.wait()
    xf = xv[...].astype(F32)
    s1 = jnp.sum(xf, axis=1, keepdims=True)
    s2 = jnp.sum(xf * xf, axis=1, keepdims=True)
    xc[...] = ((xf - s1 * (1.0 / FD)) * gain[...]).astype(BF16)
    lane = lax.broadcasted_iota(jnp.int32, (RB, 128), 1)
    st_t[...] = jnp.zeros((128, 128), F32)
    st_t[0:RB, :] = jnp.where(lane == 0, s1, jnp.where(lane == 1, s2, 0.0))
    st_grp[0] = st_t[...].T[0:8, :]
    for d in ld_t:
        d.wait()
    st_grp[0, 2:8] = jnp.full((6, 128), -1.0, F32)
    for q in range(BPD):
        st_grp[0, 2 + q : 3 + q, 0:NBR] = jnp.where(prv[q] > 0, nbv[q], -1).astype(F32)
    for d in ld_w:
        d.wait()
    g1 = gain[...].astype(BF16).astype(F32)
    g2 = (gain[...] - g1).astype(BF16).astype(F32)
    g3 = gain[...] - g1 - g2
    part_i = lax.broadcasted_iota(jnp.int32, (8, FD), 0)
    parts = jnp.where(part_i == 0, g1, jnp.where(part_i == 1, g2, jnp.where(part_i == 2, g3, 0.0)))
    parts = parts.astype(BF16)
    QC = 3 * HD
    for hf in range(2):
        gvs[hf, :, 0:QC] = jnp.sum(_dot(parts, w1q[hf]), axis=0, keepdims=True)
        gvs[hf, :, QC : QC + UC] = jnp.sum(_dot(parts, w1u[hf]), axis=0, keepdims=True)
    gm[0:1, :] = gvs[0]
    pl.semaphore_wait(barrier, len(greet))

    def slot(m, sgn, lr):
        lo = RB * (2 * sgn + lr)
        return xg.at[m, lo : lo + RB]

    def a_sem(m, sgn, lr):
        return sem_a.at[m * 4 + sgn * 2 + lr]

    def a_send(src, dst, dev):
        send(slot(*src), slot(*dst), a_sem(*dst), dev)

    def a_recv(*dst):
        recv(slot(*dst), a_sem(*dst), zp)

    for dst, dev in (((0, 0, 1), lp), ((1, 1, 0), zp), ((1, 0, 0), zm)):
        send(xc, slot(*dst), a_sem(*dst), dev)
    for k in range(1, 8):
        send(st_grp.at[0], st_grp.at[k], sem_st.at[k - 1], peers[k - 1])
    for k in range(1, 8):
        send(gvs.at[k % 2], gvg.at[k - 1], sem_g.at[k - 1], peers[k - 1])
    xg[0, 0:RB] = xc[...]
    a_recv(0, 0, 1)
    a_send((0, 0, 1), (1, 1, 1), zp)
    a_send((0, 0, 1), (1, 0, 1), zm)
    for k in range(1, 8):
        recv(st_grp.at[k], sem_st.at[k - 1], peers[k - 1])
    tot = jnp.sum(st_grp[...], axis=0) * (1.0 / DW)
    mean = tot[0:1]
    for k in range(8):
        st_own[k : k + 1] = mean - st_grp[k, 0:1] * (1.0 / FD)
    st_own[8:16] = jnp.broadcast_to(lax.rsqrt(tot[1:2] - mean * mean + 1e-06), (8, 128))
    for dev, (m, sgn, lr) in kin:
        k = m * 4 + sgn * 2 + lr
        send(st_own, st_all.at[k], sem_all.at[k], dev)
    st_all[0] = st_own[...]

    def token_of(m, j, row):
        sgn, lr = lax.shift_right_logical(j, 1), lax.bitwise_and(j, 1)
        zo = jnp.where(m == 0, 4 * sgn, jnp.where(sgn == 0, m, RINGZ - m))
        zz = lax.bitwise_and(zo + z, RINGZ - 1)
        ll = lax.bitwise_and(lr + l, 1)
        return (2 * zz + ll) * RB + row

    def blocks(k):
        b = lax.shift_right_logical(k * (65536 // RB + 1), 16)
        return b, k - b * RB

    KEYS = 4 * PB
    QROWS = 4 * RB

    def make_bias():
        enc = st_grp[...].reshape(64, 128)
        brick_id = lax.broadcasted_iota(jnp.int32, (64, 128), 1).astype(F32)
        near = jnp.full((64, 128), -1e30, F32)
        for j in range(NBR):
            near = jnp.where(enc[:, j : j + 1] == brick_id, sb_ref[c, j], near)
        key_i = lax.broadcasted_iota(jnp.int32, (1, KEYS), 1)
        kb, krow = blocks(key_i)
        kslot = lax.shift_right_logical(
            token_of(lax.shift_right_logical(kb, 2), lax.bitwise_and(kb, 3), krow), 5
        )
        eye = lax.broadcasted_iota(jnp.int32, (128, 128), 0) == lax.broadcasted_iota(
            jnp.int32, (128, 128), 1
        )
        bs_row = jnp.pad(bsv[...], ((0, 0), (0, 128 - 8 * BPD)), constant_values=-1).astype(F32)
        bs_col = jnp.sum(jnp.where(eye, bs_row, 0.0), axis=1, keepdims=True).astype(jnp.int32)
        of_key = jnp.where(bs_col == kslot, 1.0, 0.0)
        near_keys = jnp.dot(near, of_key, precision=lax.Precision.HIGHEST, preferred_element_type=F32)
        q_i = lax.broadcasted_iota(jnp.int32, (QROWS, 1), 0)
        qm, qrow = blocks(q_i)
        qm = lax.bitwise_and(4 - qm, 3)
        qslot = lax.shift_right_logical(token_of(qm, i + jnp.zeros_like(qm), qrow), 5)
        qdev = lax.shift_right_logical(qslot * (512 // BPD + 1), 9)
        qpos = 8 * lax.bitwise_and(seq + 8 - qdev, 7) + 2 + (qslot - BPD * qdev)
        of_query = jnp.where(qpos == lax.broadcasted_iota(jnp.int32, (1, 64), 1), 1.0, 0.0)
        bias[...] = jnp.dot(
            of_query, near_keys, precision=lax.Precision.HIGHEST, preferred_element_type=F32
        )

    ps, rs, po = (psq, psu), (rsq, rsu), (poq, pou)
    so, ro, ns, rn = (None, sou), (None, rou), (nsq, nsu), (rnq, rnu)
    w1 = (w1q, w1u)

    def rows(j):
        return pl.ds(pl.multiple_of(j * RB, 16), RB)

    def gather_stage(m):
        if m == 0:
            a_recv(0, 1, 0)
            a_recv(0, 1, 1)
            return
        for lr in range(2):
            for sgn in range(2):
                a_recv(m, sgn, lr)
                dev = zp if sgn == 1 else zm
                if m < 3:
                    a_send((m, sgn, lr), (m + 1, sgn, lr), dev)
                elif lr == sgn:
                    a_send((3, sgn, lr), (0, 1, lr), dev)

    def take_sums():
        for _, (m, sgn, lr) in kin:
            k = m * 4 + sgn * 2 + lr
            recv(st_all.at[k], sem_all.at[k], zp)
        for k in range(1, 8):
            recv(gvg.at[k - 1], sem_g.at[k - 1], peers[k - 1])
            gm[k : k + 1, :] = gvg[k - 1]
        for m in range(4):
            st_t[16 * m : 16 * m + 16] = st_all[4 * m + i]
        st_t[...] = st_t[...].T

    def project(p, m):
        ps[p][m] = _dot(xg[m], w1[p][1]).astype(BF16)
        send(ps[p].at[m], rs[p].at[m], sem_sib.at[p, m], sib)
        po[p][m] = _dot(xg[m], w1[p][0])
        recv(rs[p].at[m], sem_sib.at[p, m], sib)
        if p == 0:
            for d, (j, dev) in enumerate(((ip, dp), (im, dm), (io, do))):
                v = po[p][m, rows(j), :] + rs[p][m, rows(j), :].astype(F32)
                nsq[d, m] = v.astype(BF16)
                send(nsq.at[d, m], rnq.at[d, m], sem_n.at[p, d, m], dev)
            return
        so[p][m] = (po[p][m, rows(io), :] + rs[p][m, rows(io), :].astype(F32)).astype(BF16)
        send(so[p].at[m], ro[p].at[m], sem_o.at[p, m], dp if m % 2 == 0 else dm)

    def relay(p, m):
        recv(ro[p].at[m], sem_o.at[p, m], dp)
        for d, (j, dev) in enumerate(((ip, dp), (im, dm))):
            v = po[p][m, rows(j), :] + rs[p][m, rows(j), :].astype(F32)
            if d == m % 2:
                v = v + ro[p][m].astype(F32)
            ns[p][d, m] = v.astype(BF16)
            send(ns[p].at[d, m], rn[p].at[d, m], sem_n.at[p, d, m], dev)

    def reduced(p, m):
        v = po[p][m, rows(i), :] + rs[p][m, rows(i), :].astype(F32)
        for d in range(2 if p else 3):
            recv(rn[p].at[d, m], sem_n.at[p, d, m], dp)
            v = v + rn[p][d, m].astype(F32)
        v = v - jnp.dot(
            st_t[0:RB, 16 * m : 16 * m + 8], gm[:, p * QC : p * QC + v.shape[1]],
            precision=lax.Precision.HIGHEST, preferred_element_type=F32,
        )
        return v * st_t[0:RB, 16 * m + 8 : 16 * m + 9]

    def kv_rows(m, j):
        return kvb.at[pl.ds(pl.multiple_of(m * PB + j * RB, 16), RB)]

    def finish_qkv(m):
        v = reduced(0, m).astype(BF16)
        at = (4 - m) % 4 * RB
        qb[at : at + RB] = v[:, 0:HD]
        own = kv_rows(m, i)
        own[...] = v[:, HD:]
        send(own, own, sem_kv.at[m, 0], dp)
        send(own, own, sem_kv.at[m, 1], dm)
        send(own, own, sem_kv.at[m, 2], do)

    span = ((0, HD), (HD, AH))

    def j_part(hf, part, m, j):
        return jb.at[hf, m, rows(j), span[part][0] : span[part][1]]

    def spread(part, m):
        own = j_part(0, part, m, i)
        send(own, own, sem_d.at[part, m, 0], dp)
        send(own, own, sem_d.at[part, m, 1], dm)
        send(own, j_part(1, part, m, i), sem_df.at[part, m, 0], sib)

    def spread_relay(part, m):
        for d, j in enumerate((im, ip)):
            got = j_part(0, part, m, j)
            recv(got, sem_d.at[part, m, d], dp)
            if d == m % 2:
                send(got, got, sem_d.at[part, m, 2], dp if d == 0 else dm)
            send(got, j_part(1, part, m, j), sem_df.at[part, m, 1 + d], sib)

    def spread_last(part, m):
        got = j_part(0, part, m, io)
        recv(got, sem_d.at[part, m, 2], dp)
        send(got, j_part(1, part, m, io), sem_df.at[part, m, 3], sib)

    def spread_sib(part, m):
        for k, j in enumerate((i, im, ip, io)):
            recv(j_part(1, part, m, j), sem_df.at[part, m, k], sib)

    def finish_up(m):
        u = reduced(1, m)
        h = u * (1.0 + lax.erf(u * (1.0 / math.sqrt(2.0)))) * 0.5
        jb[0, m, rows(i), HD:AH] = h.astype(BF16)
        spread(1, m)

    def attend():
        for m in range(4):
            for d, j in enumerate((im, ip, io)):
                recv(kv_rows(m, j), sem_kv.at[m, d], dp)
        for two in ((0, 3), (2, 1)):
            lo = (4 - two[0]) % 4 * RB
            s = lax.dot_general(
                qb[lo : lo + 2 * RB], kvb[:, 0:HD], (((1,), (1,)), ((), ())),
                preferred_element_type=F32,
            )
            s = s * (HD**-0.5) + bias[lo : lo + 2 * RB, :]
            e = jnp.exp(s - jnp.max(s, axis=1, keepdims=True))
            total = jnp.sum(e, axis=1, keepdims=True)
            a = (_dot(e.astype(BF16), kvb[:, HD:]) / total).astype(BF16)
            for n, m in enumerate(two):
                jb[0, m, rows(i), 0:HD] = a[n * RB : (n + 1) * RB]
                spread(0, m)

    halves = [(h, slice(h * CO // 2, (h + 1) * CO // 2)) for h in range(2)]

    def contribute(m):
        for part in range(2):
            spread_last(part, m)
        fbuf[m] = _dot(jb[0, m], w2[0])
        for part in range(2):
            spread_sib(part, m)
        fbuf[m] += _dot(jb[1, m], w2[1])
        if m == 0:
            es3[...] = fbuf[0, 2 * RB :].astype(BF16)
            for h, cs in halves:
                for lr, dev in ((0, zp), (1, zm)):
                    blk = slice(lr * RB, (lr + 1) * RB)
                    send(es3.at[blk, cs], er.at[3, lr, blk, cs], sem_e.at[3, lr, h], dev)
            lsnd[...] = fbuf[0, RB : 2 * RB].astype(BF16)
            send(lsnd, lrcv, sem_l, lp)
            fown[...] = xv[...].astype(F32) + fbuf[0, 0:RB]
            return
        for h, cs in halves:
            for sgn, dev, far in ((0, zp, zpo), (1, zm, zmo)):
                lo = 2 * RB * sgn
                if m == 3:
                    a, b = sgn * RB, RB - sgn * RB
                    got = er.at[3, sgn, a : a + RB, cs]
                    recv(got, sem_e.at[3, sgn, h], dev)
                    es[2, sgn, a : a + RB, cs] = (
                        fbuf[3, lo + a : lo + a + RB, cs] + got[...].astype(F32)
                    ).astype(BF16)
                    es[2, sgn, b : b + RB, cs] = fbuf[3, lo + b : lo + b + RB, cs].astype(BF16)
                else:
                    got = er.at[m, sgn, :, cs]
                    recv(got, sem_e.at[m, sgn, h], dev)
                    es[m - 1, sgn, :, cs] = (
                        fbuf[m, lo : lo + 2 * RB, cs] + got[...].astype(F32)
                    ).astype(BF16)
                if m > 1:
                    send(
                        es.at[m - 1, sgn, :, cs], er.at[m - 1, sgn, :, cs],
                        sem_e.at[m - 1, sgn, h], dev,
                    )
                else:
                    for lr, to in ((1, far), (0, dev)):
                        send(
                            es.at[0, sgn, lr * RB : (lr + 1) * RB, cs],
                            fin.at[sgn, lr, :, cs], sem_f.at[sgn, lr, h], to,
                        )

    def last():
        recv(lrcv, sem_l, lp)
        for h, cs in halves:
            v = fown[:, cs] + lrcv[:, cs].astype(F32)
            for lr in range(2):
                for sgn in range(2):
                    recv(fin.at[sgn, lr, :, cs], sem_f.at[sgn, lr, h], zp)
                    v = v + fin[sgn, lr, :, cs].astype(F32)
            res[:, cs] = v.astype(BF16)
            if SECT > 1:
                send(res.at[:, cs], o_ref.at[:, cs], sem_sec.at[h], sec_next)
            else:
                d = pltpu.make_async_copy(res.at[:, cs], o_ref.at[:, cs], sem_loc.at[0])
                d.start()
                d.wait()

    gather_stage(1)
    project(0, 1)
    gather_stage(2)
    project(0, 2)
    make_bias()
    take_sums()
    gather_stage(3)
    project(0, 3)
    finish_qkv(1)
    gather_stage(0)
    project(0, 0)
    finish_qkv(2)
    project(1, 0)
    finish_qkv(3)
    project(1, 3)
    finish_qkv(0)
    relay(1, 0)
    project(1, 2)
    relay(1, 3)
    attend()
    finish_up(0)
    project(1, 1)
    relay(1, 2)
    finish_up(3)
    for d in ld_w2:
        d.wait()
    spread_relay(0, 0)
    spread_relay(0, 3)
    relay(1, 1)
    spread_relay(1, 0)
    finish_up(2)
    spread_relay(0, 2)
    spread_relay(0, 1)
    finish_up(1)
    spread_relay(1, 3)
    contribute(0)
    spread_relay(1, 2)
    contribute(3)
    spread_relay(1, 1)
    contribute(2)
    contribute(1)
    last()
    for d in sends:
        d.wait_send()
    if SECT > 1:
        for h, cs in halves:
            recv(o_ref.at[:, cs], sem_sec.at[h], sec_next)


def per_device(sect, x, gain, qkv, up, out, down, sb, nb, pr, bs):
    RB, FD = x.shape[1:]
    UC = up.shape[2] // 2
    CO = out.shape[2]
    BPD = nb.shape[1]
    AH = HD + UC
    PB = CHIPS * RB
    QC = 3 * HD
    dims = (RB, FD, UC, CO, BPD, FD * 8, sect)
    vm, sm = pltpu.VMEM, pltpu.SemaphoreType.DMA
    scratch = [
        vm((RB, FD), BF16), vm((1, FD), F32), vm((2, FD, QC), BF16), vm((2, FD, UC), BF16),
        vm((2, AH, CO), BF16),
        vm((BPD, 1, NBR), jnp.int32), vm((BPD, 1, NBR), jnp.int32), vm((1, 8 * BPD), jnp.int32),
        vm((128, 128), F32), vm((8, 8, 128), F32), vm((16, 128), F32), vm((16, 16, 128), F32),
        vm((4 * RB, 4 * PB), F32),
        vm((4, PB, FD), BF16), vm((2, 1, QC + UC), F32), vm((7, 1, QC + UC), F32), vm((8, QC + UC), F32),
        vm((RB, FD), BF16),
    ]
    two = (QC, UC)
    scratch += [vm((4, PB, w), BF16) for w in two]
    scratch += [vm((4, PB, w), BF16) for w in two]
    scratch += [vm((4, PB, w), F32) for w in two]
    scratch += [vm((4, RB, UC), BF16) for _ in range(2)]
    scratch += [vm((n, 4, RB, w), BF16) for n, w in ((3, QC), (2, UC))]
    scratch += [vm((n, 4, RB, w), BF16) for n, w in ((3, QC), (2, UC))]
    scratch += [
        vm((4 * RB, HD), BF16), vm((4 * PB, 2 * HD), BF16), vm((2, 4, PB, AH), BF16),
        vm((RB, CO), F32), vm((4, PB, CO), F32), vm((2 * RB, CO), BF16), vm((3, 2, 2 * RB, CO), BF16),
        vm((4, 2, 2 * RB, CO), BF16), vm((2, 2, RB, CO), BF16), vm((RB, CO), BF16), vm((RB, CO), BF16), vm((RB, CO), BF16),
        sm((20,)), sm((7, 2)), sm((7, 2)), sm((16, 2)), sm((16, 2)), sm((2, 4, 2)), sm((2, 4, 2)),
        sm((2, 3, 4, 2)), sm((4, 3, 2)), sm((2, 4, 3, 2)), sm((2, 4, 4, 2)), sm((4, 2, 2, 2)),
        sm((2, 2, 2, 2)), sm((2,)), sm((2, 2)),
    ]
    hbm = pl.BlockSpec(memory_space=pl.ANY)
    y = pl.pallas_call(
        functools.partial(kernel, dims),
        out_shape=jax.ShapeDtypeStruct((RB, CO), BF16),
        in_specs=[hbm] * 9 + [pl.BlockSpec(memory_space=pltpu.SMEM)],
        out_specs=hbm,
        scratch_shapes=scratch,
        compiler_params=pltpu.CompilerParams(
            collective_id=0, has_side_effects=True, vmem_limit_bytes=56 * 2**20
        ),
    )(
        x[0], gain, jnp.transpose(qkv[0], (1, 0, 2)), up[0], out[0], down[0],
        jnp.transpose(nb, (1, 0, 2)), jnp.transpose(pr, (1, 0, 2)), bs, sb[0],
    )
    return y[None]


def solution(mesh):
    return jax.shard_map(
        functools.partial(per_device, mesh.shape["section"]),
        mesh=mesh,
        in_specs=(
            P("section", "tensor", "seq"),
            P("section", "seq"),
            P("section", "seq", None, "tensor"),
            P("section", "seq", "tensor"),
            P("section", "tensor", "seq"),
            P("section", "tensor", "seq"),
            P("section", "tensor", None),
            P("section", "seq", None),
            P("section", "seq", None),
            P("section", None),
        ),
        out_specs=P("section", "tensor", "seq"),
        check_vma=False,
    )
```

time: 105 us -> 99.6 us (0.949)
  Pallas kernels: 104 us -> 97.9 us
    pallas_call x1, Pallas kernels: 104 us -> 97.9 us  [per_device(): pl.pallas_call(functools.partial(kernel, dims), out_shape=jax.ShapeDtypeS...]
where the time goes in v2:
time: 99.6 us; the launch traced here: 99.4 us
  Pallas kernels  97.9 us (98%)
  local copies, waits for them, and re-layouts  1.52 us (2%)
    pallas_call x1, Pallas kernels, per_device(): pl.pallas_call(functools.partial(kernel, dims), out_shape=jax.ShapeDtypeS...  97.9 us

profile of v2, /device:TPU:16, one launch (start us, length us, event | category | flops | bytes accessed | tf_op | source)
XLA Modules:
  0.0 99.4 jit_solution(9094184597703870344)
XLA Ops:
  0.0 97.9 %shard_map.100 = bf16[48,768]{1,0:T(8,128)(2,1)} custom-call(bf16[48,768]{1,0:T(8,128)(2,1)} %bitcast.16, f32[1,768]{1,0:T(1,128)} %gain_in.1, bf16[3,768,256]{2,1,0:T(8,128)(2,1)} %bitcast.11, bf16[768,768]{1,0:T(8,128)(2,1)} %bitcast.12, bf16[256,768]{1,0:T(8,128)(2,1)} %bitcast.14, bf16[768,768]{1,0:T(8,128)(2,1)} %bitcast.13, s32[3,1,27]{2,1,0:T(1,128)} %bitcast.17, ...), custom_call_target="tpu_custom_call" | custom-call | tf_op jit(solution)/shard_map/pallas_call | solution.py:502
  97.9 1.5 %copy.12 = bf16[1,48,768]{2,1,0:T(8,128)(2,1)} copy(bf16[1,48,768]{2,1,0:T(8,128)(2,1)} %bitcast.15) | data formatting | bytes 147456
